TPU v7x, 512 devices: a whole 4x8x8 slice. The times are simulated.
512 devices in a mesh: dp: 64 (over x, z, core), graph: 8 (over y).
Axes of the slice: x: 4, y: 8, z: 8, core: 2. Of those that a mesh axis runs over, the one named last changes fastest.
Arguments:
- texts: bfloat16 [2048, 128, 768], P(('dp', 'graph')), may hold values from -48 to 48
- qkv_weight: bfloat16 [768, 2304], P(None, 'dp'), may hold values from -0.21875 to 0.21875
- norm_gain: float32 [768], replicated, may hold values from 0.1 to 1.9
- routes: int32 [2048, 8], P(('dp', 'graph')), may hold values from 0 to 63, all different within a row; in each aligned block of 4 rows (0 to 3, 4 to 7, ...) at most 2 rows name the same one
- w_self: float32 [768, 1024], P(None, 'graph'), may hold values from -0.21875 to 0.21875
- w_neigh: float32 [768, 1024], P(None, 'graph'), may hold values from -0.21875 to 0.21875
- gnn_bias: float32 [1024], P('graph'), may hold values from -3 to 3
- neighbors: int32 [65536, 15], P('dp'), may hold values from 0 to 1023
- cotangent: float32 [65536, 1024], P('dp', 'graph'), may hold values from -6 to 6
Outputs:
- hidden_nodes: float32 [65536, 1024], P('dp', 'graph')
- node_grads: float32 [2048, 768], P(('dp', 'graph'))
Inputs may be any that keep to these rules, and one draw needn't show every extreme that they name: `routes`: in each aligned block of 4 rows no partition is named more than 2 times, and a row never names a partition twice.
All inputs are finite; a program needn't handle non-finite values.
Results may differ from a plain program's by a relative error of at most 0.012.
The roundings to bfloat16 on the way count: a program that leaves them out, or rounds other values in their place, can miss the bound.
Values may be sent and summed in bfloat16 or wider, within the bound.
A program may use at most 64 MiB of HBM per device.

v0:
```python
import math

import jax
import jax.numpy as jnp
from jax import lax
from jax.sharding import PartitionSpec as P

HEADS = 12


def shards(texts, qkv_weight, norm_gain, routes, w_self, w_neigh, gnn_bias, neighbors, cotangent):
    titles, length, width = texts.shape
    head_count = HEADS
    head_size = width // head_count
    part_count = lax.axis_size("dp")
    copies = routes.shape[1]
    capacity = max(2, (copies * titles + part_count - 1) // part_count)
    flat_rows = texts.reshape(titles * length, width)
    projected = jnp.dot(
        flat_rows,
        lax.all_gather(qkv_weight, "dp", axis=1, tiled=True),
        preferred_element_type=jnp.float32,
    ).astype(jnp.bfloat16)
    projected = projected.reshape(titles, length, 3, head_count, head_size)
    scores = jnp.einsum(
        "tqhd,tkhd->thqk",
        projected[:, :, 0],
        projected[:, :, 1],
        preferred_element_type=jnp.float32,
    ) / math.sqrt(head_size)
    probs = jax.nn.softmax(scores, axis=-1).astype(jnp.bfloat16)
    attended = jnp.einsum(
        "thqk,tkhd->tqhd", probs, projected[:, :, 2], preferred_element_type=jnp.float32
    )
    pooled = jnp.mean(attended, axis=1).reshape(titles, width)
    center = jnp.mean(pooled, axis=1, keepdims=True)
    spread = jnp.mean((pooled - center) ** 2, axis=1, keepdims=True)
    features = ((pooled - center) / jnp.sqrt(spread + 1e-05) * norm_gain).astype(jnp.bfloat16)
    targets = routes.reshape(-1)
    onehot = (targets[:, None] == jnp.arange(part_count, dtype=jnp.int32)[None, :]).astype(
        jnp.int32
    )
    before = jnp.cumsum(onehot, axis=0) - onehot
    slot_rank = jnp.sum(before * onehot, axis=1)
    position = targets * capacity + slot_rank
    placer = (
        jnp.arange(part_count * capacity, dtype=jnp.int32)[:, None] == position[None, :]
    ).astype(jnp.bfloat16)
    copied = jnp.repeat(features, copies, axis=0)
    outgoing = jnp.dot(placer, copied, preferred_element_type=jnp.float32).astype(jnp.bfloat16)
    outgoing = outgoing.reshape(part_count, capacity, width)
    w_both = jnp.concatenate([w_self, w_neigh], axis=1)
    received = lax.all_to_all(outgoing, "dp", split_axis=0, concat_axis=0, tiled=True).reshape(
        -1, width
    )
    mixed_rows = jnp.dot(
        lax.all_gather(received, "graph", axis=0, tiled=True).astype(jnp.float32),
        w_both,
        precision=lax.Precision.HIGHEST,
        preferred_element_type=jnp.float32,
    )
    hid_cols = w_self.shape[1]
    row_total = mixed_rows.shape[0]
    self_part = mixed_rows[:, :hid_cols]
    neigh_part = mixed_rows[:, hid_cols:]
    row_numbers = jnp.arange(row_total, dtype=jnp.int32)
    adjacency = jnp.sum(
        (neighbors[:, :, None] == row_numbers[None, None, :]).astype(jnp.float32), axis=1
    )
    neighbor_sum = jnp.dot(
        adjacency, neigh_part, precision=lax.Precision.HIGHEST, preferred_element_type=jnp.float32
    )
    preact = self_part + neighbor_sum + gnn_bias
    gate_sig = jax.nn.sigmoid(preact)
    hidden = preact * gate_sig
    pre_grad = cotangent * gate_sig * (1.0 + preact * (1.0 - gate_sig))
    back = lax.dot_general(
        adjacency,
        pre_grad,
        (((0,), (0,)), ((), ())),
        precision=lax.Precision.HIGHEST,
        preferred_element_type=jnp.float32,
    )
    joined = jnp.concatenate([pre_grad, back], axis=1)
    own_slab = lax.psum_scatter(
        jnp.dot(
            joined, w_both.T, precision=lax.Precision.HIGHEST, preferred_element_type=jnp.float32
        ),
        "graph",
        scatter_dimension=0,
        tiled=True,
    )
    returned = lax.all_to_all(
        own_slab.reshape(part_count, capacity, width), "dp", split_axis=0, concat_axis=0, tiled=True
    )
    returned = returned.reshape(part_count * capacity, width)
    per_copy = jnp.dot(
        placer.astype(jnp.float32).T,
        returned,
        precision=lax.Precision.HIGHEST,
        preferred_element_type=jnp.float32,
    )
    node_grads = jnp.sum(per_copy.reshape(titles, copies, width), axis=1)
    return (hidden, node_grads)


def solution(mesh):
    placed = (
        P(("dp", "graph"), None, None),
        P(None, "dp"),
        P(),
        P(("dp", "graph"), None),
        P(None, "graph"),
        P(None, "graph"),
        P("graph"),
        P("dp", None),
        P("dp", "graph"),
    )
    return jax.shard_map(
        shards,
        mesh=mesh,
        in_specs=placed,
        out_specs=(P("dp", "graph"), P(("dp", "graph"), None)),
        check_vma=False,
    )
```

profile of v0, /device:TPU:1, one launch (start us, length us, event | category | flops | bytes accessed | tf_op | source)
XLA Modules:
  0.0 284.3 jit_solution(6417935240890173218)
XLA Ops:
  7.2 0.7 all-gather.6.cloned.1.call-update
  8.0 0.8 reshape.89
  9.0 92.7 %all-gather.6.cloned.1.call-done = bf16[64,36,768]{2,1,0:T(8,128)(2,1)} async-done(((bf16[1,36,768]{2,1,0:T(8,128)(2,1)}), bf16[64,36,768]{2,1,0:T(8,128)(2,1)}) %all-gather.6.cloned.1.call-update) | async-done | bytes 3538960 | tf_op jit(solution)/shard_map/all_gather | solution.py:21
  101.8 6.2 %reshape.98 = bf16[2304,768]{1,0:T(8,128)(2,1)} reshape(bf16[64,36,768]{2,1,0:T(8,128)(2,1)} %all-gather.6.cloned.1.call-done) | data formatting | bytes 7077888
  108.0 4.0 %convolution_convert_fusion = bf16[512,2304]{1,0:T(8,128)(2,1)S(1)} fusion(bf16[512,768]{1,0:T(8,128)(2,1)S(1)} %bitcast.30, bf16[2304,768]{1,0:T(8,128)(2,1)} %reshape.98), kind=kOutput, calls=%fused_computation.3 | convolution fusion | flops 1813118976 | bytes 6684672 | tf_op jit(solution)/shard_map/dot_general | solution.py:19
  112.0 2.5 copy.34
  114.4 4.2 %reshape.91 = bf16[4,128,3,12,64]{1,0,4,3,2:T(4,128)(2,1)S(1)} reshape(bf16[512,2304]{0,1:T(8,128)(2,1)} %copy.34) | data formatting | bytes 4718592 | tf_op jit(solution)/shard_map/reshape | solution.py:24
  118.6 0.9 fusion.25
  120.1 3.0 %fusion.26 = (f32[4,12,128]{2,1,0:T(8,128)S(1)}, f32[4,12,128,128]{2,3,1,0:T(8,128)S(1)}) fusion(f32[4,12,128,128]{2,3,1,0:T(8,128)S(1)} %fusion.12), kind=kOutput, calls=%fused_computation.49 | output fusion | flops 3145855 | bytes 6316032 | tf_op jit(solution)/shard_map/sub | solution.py:31
  123.2 0.6 fusion.6
  124.7 17.4 %all_to_all.10 = bf16[64,2,768]{2,1,0:T(2,128)(2,1)S(1)} all-to-all(bf16[64,2,768]{2,1,0:T(2,128)(2,1)S(1)} %reshape.93), channel_id=1, replica_groups=mesh['dp'=64,'graph'=8] {'dp'}, dimensions={0} | all-to-all | bytes 393216 | tf_op jit(solution)/shard_map/all_to_all | solution.py:53
  142.0 0.8 reshape.94
  143.2 9.5 %convert_reduce_fusion = f32[1024,1024]{1,0:T(8,128)} fusion(s32[1024,15]{0,1:T(8,128)S(1)} %copy-done.5), kind=kLoop, calls=%fused_computation.1 | loop fusion | flops 46137344 | bytes 4255744 | tf_op jit(solution)/shard_map/reduce_sum | solution.py:67
  152.7 24.6 %all-gather.4.cloned.1.call-done = bf16[1024,768]{1,0:T(8,128)(2,1)} async-done(((bf16[128,768]{1,0:T(8,128)(2,1)}), bf16[1024,768]{1,0:T(8,128)(2,1)}) %all-gather.4.cloned.1.call-update) | async-done | bytes 1572880 | tf_op jit(solution)/shard_map/all_gather | solution.py:57
  177.4 2.8 fusion.27
  180.2 6.9 %add_multiply_fusion = (f32[1024,128]{0,1:T(8,128)S(1)}, f32[1024,128]{0,1:T(8,128)S(1)}) fusion(f32[1024,128]{0,1:T(8,128)S(1)} %copy.39, f32[128]{0:T(128)S(1)} %copy-done.7, f32[1024,1024]{1,0:T(8,128)} %convert_reduce_fusion, f32[1024,256]{0,1:T(8,128)S(1)} %fusion.27), kind=kOutput, calls=%fused_computation.24 | convolution fusion | flops 1612054528 | bytes 6816256 | tf_op jit(solution)/shard_map/dot_general | solution.py:70
  187.1 2.4 fusion.28
  189.6 7.2 %fusion.8 = f32[1024,768]{1,0:T(8,128)} fusion(f32[768,256]{1,0:T(8,128)S(1)} %constant_dynamic-update-slice_fusion, f32[1024,128]{0,1:T(8,128)S(1)} %fusion.28, f32[1024,128]{0,1:T(8,128)S(1)} %get-tuple-element.13), kind=kOutput, calls=%fused_computation.15 | convolution fusion | flops 2416181248 | bytes 4980736 | tf_op jit(solution)/shard_map/dot_general | solution.py:86
  196.7 49.6 %reduce-scatter.2.cloned.1.call-done = f32[128,768]{1,0:T(8,128)} async-done(((f32[1024,768]{1,0:T(8,128)}), f32[128,768]{1,0:T(8,128)}) %reduce-scatter.2.cloned.1.call-update) | async-done | bytes 393232 | tf_op jit(solution)/shard_map/reduce_scatter | solution.py:85
  246.4 2.0 reshape.95
  248.3 13.7 %all-to-all-start.1 = ((f32[64,2,768]{2,1,0:T(2,128)}), f32[64,2,768]{2,1,0:T(2,128)S(1)}, u32[]{:S(2)}, u32[]{:S(2)}) async-start(f32[64,2,768]{2,1,0:T(2,128)} %reshape.95), calls=%async_computation.2 | async-start | bytes 786432 | tf_op jit(solution)/shard_map/all_to_all | solution.py:93
  262.0 1.0 copy.40
  263.0 13.6 %all-to-all-done.1 = f32[64,2,768]{2,1,0:T(2,128)S(1)} async-done(((f32[64,2,768]{2,1,0:T(2,128)}), f32[64,2,768]{2,1,0:T(2,128)S(1)}, u32[]{:S(2)}, u32[]{:S(2)}) %all-to-all-start.1) | async-done | bytes 393248 | tf_op jit(solution)/shard_map/all_to_all | solution.py:93
  276.9 0.9 convolution_reduce_fusion
  (38 shorter events, 2.4 us)
Async XLA Ops:
  7.2 100.8 %copy-start = (bf16[4,128,768]{2,1,0:T(8,128)(2,1)S(1)}, bf16[4,128,768]{2,1,0:T(8,128)(2,1)}, u32[]{:S(2)}) copy-start(bf16[4,128,768]{2,1,0:T(8,128)(2,1)} %param.9) | copy-start | bytes 2359300
  7.2 94.6 %all-gather.6.cloned.1.call-start = ((), (), s32[]{:S(2)}) async-start(), calls=%async_computation.5 | async-start | bytes 3993600 | tf_op jit(solution)/shard_map/all_gather | solution.py:21
  7.9 169.5 %all-gather.4.cloned.1.call-start = ((), (), s32[]{:S(2)}) async-start(), calls=%async_computation.3 | async-start | bytes 1769472 | tf_op jit(solution)/shard_map/all_gather | solution.py:57
  123.2 1.1 copy-start.6
  123.2 19.7 %copy-start.2 = (f32[1024,128]{1,0:T(8,128)S(1)}, f32[1024,128]{1,0:T(8,128)}, u32[]{:S(2)}) copy-start(f32[1024,128]{1,0:T(8,128)} %param.17) | copy-start | bytes 1572868
  123.2 19.9 %copy-start.3 = (f32[768,128]{1,0:T(8,128)S(1)}, f32[768,128]{1,0:T(8,128)}, u32[]{:S(2)}) copy-start(f32[768,128]{1,0:T(8,128)} %param.13) | copy-start | bytes 1179652
  123.9 19.2 %copy-start.4 = (f32[768,128]{1,0:T(8,128)S(1)}, f32[768,128]{1,0:T(8,128)}, u32[]{:S(2)}) copy-start(f32[768,128]{1,0:T(8,128)} %param.14) | copy-start | bytes 1179652
  123.9 19.3 %copy-start.5 = (s32[1024,15]{0,1:T(8,128)S(1)}, s32[1024,15]{0,1:T(8,128)}, u32[]{:S(2)}) copy-start(s32[1024,15]{0,1:T(8,128)} %param.16) | copy-start | bytes 184324
  142.8 103.6 %reduce-scatter.2.cloned.1.call-start = ((), (), s32[]{:S(2)}) async-start(), calls=%async_computation.4 | async-start | bytes 3538944 | tf_op jit(solution)/shard_map/reduce_scatter | solution.py:85
  143.2 37.0 %copy-start.7 = (f32[128]{0:T(128)S(1)}, f32[128]{0:T(128)}, u32[]{:S(2)}) copy-start(f32[128]{0:T(128)} %param.15) | copy-start | bytes 1540
  180.2 6.9 %copy-start.1 = (f32[1024,1024]{1,0:T(8,128)S(1)}, f32[1024,1024]{1,0:T(8,128)}, u32[]{:S(2)}) copy-start(f32[1024,1024]{1,0:T(8,128)} %convert_reduce_fusion) | copy-start | bytes 12582916
  248.3 28.3 %all-to-all-start.1 = ((f32[64,2,768]{2,1,0:T(2,128)}), f32[64,2,768]{2,1,0:T(2,128)S(1)}, u32[]{:S(2)}, u32[]{:S(2)}) async-start(f32[64,2,768]{2,1,0:T(2,128)} %reshape.95), calls=%async_computation.2 | async-start | bytes 786432 | tf_op jit(solution)/shard_map/all_to_all | solution.py:93
Sparse Core Ops, SparseCore 0:
  11.3 90.4 all-gather.5
  142.9 34.3 all-gather.3
  196.9 49.4 reduce-scatter.1
where the time goes:
time: 285 us; the launch traced here: 284 us
  waiting for transfers between devices  181 us (64%)
  matrix products  25.7 us (9%)
  local copies, waits for them, and re-layouts  18.9 us (7%)
  blocking collectives  17.4 us (6%)
  between operations  14 us (5%)
  starting transfers between devices  13.8 us (5%)
  other arithmetic  13.3 us (5%)
    all_gather x1, waiting for transfers between devices, shards(): lax.all_gather(qkv_weight, 'dp', axis=1, tiled=True)  92.7 us
    reduce_scatter x1, waiting for transfers between devices, shards(): lax.psum_scatter(jnp.dot(joined, w_both.T, precision=lax.Precision.HIGHES...  49.6 us
    all_gather x1, waiting for transfers between devices, shards(): lax.all_gather(received, 'graph', axis=0, tiled=True).astype(jnp.float32)  24.6 us
    all_to_all x1, blocking collectives, shards(): lax.all_to_all(outgoing, 'dp', split_axis=0, concat_axis=0, tiled=True)  17.4 us
    all_to_all x1, starting transfers between devices, shards(): lax.all_to_all(own_slab.reshape(part_count, capacity, width), 'dp', split...  13.7 us
    all_to_all x1, waiting for transfers between devices, shards(): lax.all_to_all(own_slab.reshape(part_count, capacity, width), 'dp', split...  13.6 us
    reduce_sum x1, other arithmetic, shards(): jnp.sum((neighbors[:, :, None] == row_numbers[None, None, :]).astype(jnp....  9.54 us
    unnamed x20, local copies, waits for them, and re-layouts  7.44 us
  transfers between devices with their start and end apart: 4, of which 4 were waited for; matrix products, arithmetic and copies ran while one was open for 4% of the time, Pallas kernels for 0%

commit v1 on v0

v1 whole, which is shorter than its diff:
```python
import functools

import jax
import jax.numpy as jnp
from jax import lax
from jax.experimental import pallas as pl
from jax.experimental.pallas import tpu as pltpu
from jax.sharding import PartitionSpec as P

NX, NZ, NC, NY = 4, 8, 2, 8
D = 768
HALF = 384
TITLES = 4
SEQ = 128
COLS = 256
ROWS = 1024
FAN = 15
BF16 = jnp.bfloat16
F32 = jnp.float32
NT = (((1,), (1,)), ((), ()))
NN = (((1,), (0,)), ((), ()))


def dot(a, b, dims=NN):
    return lax.dot_general(a, b, dims, preferred_element_type=F32)


def split(value):
    high = value.astype(BF16)
    return high, (value - high.astype(F32)).astype(BF16)


def iota(shape, axis):
    return lax.broadcasted_iota(jnp.int32, shape, axis)


def kernel(
    texts, wt, gain, routes, w_self, w_neigh, bias, near, cot,
    hidden_out, grads_out,
    wa, wb, dense, qkv, pooled, adj_t, adj, w_hi, w_lo,
    ry, rt, sel, sel_t, feats, tg, xs, ds, ub, ur, vs, vr, yo, yr, po, pr,
    sa_x, ra_x, sa_z, ra_z, sa_d, ra_d, sb_z, rb_z, sb_x, rb_x, sb_d, rb_d,
    sr_y, rr_y, sr_z, rr_z, sr_x, rr_x, sr_d, rr_d,
    sf, rf, st_z, rt_z, st_x, rt_x, st_d, rt_d,
    su_d, ru_d, su_x, ru_x, su_z, ru_z, sp, rp,
):
    dp = lax.axis_index("dp")
    y = lax.axis_index("graph")
    x = dp // 16
    z = (dp // 2) % 8
    c = dp % 2
    other = 1 - c

    def at(px, pz, pc, py):
        return (px * 16 + pz * 2 + pc, py)

    def xp(k):
        return at((x + k) % NX, z, c, y)

    def zp(k):
        return at(x, (z + k) % NZ, c, y)

    def yp(k):
        return at(x, z, c, (y + k) % NY)

    mate = at(x, z, other, y)

    def send(src, dst, ssem, rsem, peer):
        return pltpu.make_async_remote_copy(
            src_ref=src, dst_ref=dst, send_sem=ssem, recv_sem=rsem,
            device_id=peer, device_id_type=pl.DeviceIdType.MESH,
        )

    def loop(low, high, body):
        def step(i, carry):
            body(i)
            return carry
        lax.fori_loop(low, high, step, 0)

    def a_x(k):
        return send(wa.at[c, z, x], wa.at[c, z, x], sa_x.at[k], ra_x.at[k], xp(k))

    def a_z(step, way):
        hops = step if way == 0 else -step
        chunk = (z - hops + NZ) % NZ
        part = wa.at[c, chunk]
        if step == 3:
            part = part.at[pl.ds(2 * way, 2)]
        peer = zp(1) if way == 0 else zp(NZ - 1)
        return send(part, part, sa_z.at[step, way], ra_z.at[step, way], peer)

    def a_d(step, way):
        hops = step if way == 0 else -step
        chunk = (z - hops + NZ) % NZ
        part = wa.at[c, chunk]
        if step == 4:
            part = part.at[pl.ds(2 * way, 2)]
        return send(part, part, sa_d.at[step, way], ra_d.at[step, way], mate)

    def b_z(k):
        return send(wb.at[c, x, z], wb.at[c, x, z], sb_z.at[k], rb_z.at[k], zp(k))

    def b_x(k):
        return send(wb.at[c, x], wb.at[c, x], sb_x.at[k], rb_x.at[k], xp(k))

    def b_d(k):
        part = wb.at[c, (x - k + NX) % NX]
        return send(part, part, sb_d.at[k], rb_d.at[k], mate)

    def r_y(k):
        return send(ry.at[y], ry.at[y], sr_y.at[k], rr_y.at[k], yp(k))

    def r_z(k):
        return send(rt.at[x, c, z], rt.at[x, c, z], sr_z.at[k], rr_z.at[k], zp(k))

    def r_x(k):
        return send(rt.at[x, c], rt.at[x, c], sr_x.at[k], rr_x.at[k], xp(k))

    def r_d(k):
        part = rt.at[(x - k + NX) % NX, c]
        return send(part, part, sr_d.at[k], rr_d.at[k], mate)

    def f_y(k):
        return send(feats.at[y], feats.at[y], sf.at[k], rf.at[k], yp(k))

    def t_z(k):
        return send(tg.at[x, c, z], tg.at[x, c, z], st_z.at[k], rt_z.at[k], zp(k))

    def t_x(k):
        return send(tg.at[x, c], tg.at[x, c], st_x.at[k], rt_x.at[k], xp(k))

    def t_d(k):
        part = tg.at[(x - k + NX) % NX, c]
        return send(part, part, st_d.at[k], rt_d.at[k], mate)

    def u_d(k):
        to = (x + k) % NX
        return send(ub.at[to, other], ur.at[to], su_d.at[k], ru_d.at[k], mate)

    def u_x(k):
        return send(vs.at[(x + k) % NX], vr.at[k], su_x.at[k], ru_x.at[k], xp(k))

    def u_z(k):
        return send(yo.at[(z + k) % NZ], yr.at[k], su_z.at[k], ru_z.at[k], zp(k))

    def p_y(k):
        return send(po.at[(y + k) % NY], pr.at[k], sp.at[k], rp.at[k], yp(k))

    barrier = pltpu.get_barrier_semaphore()

    def greet(peer):
        pl.semaphore_signal(barrier, inc=1, device_id=peer, device_id_type=pl.DeviceIdType.MESH)

    greet(mate)
    loop(1, NX, lambda k: greet(xp(k)))
    loop(1, NZ, lambda k: greet(zp(k)))
    loop(1, NY, lambda k: greet(yp(k)))

    wa[c, z, x] = wt[:, :HALF]
    wb[c, x, z] = wt[:, HALF:]
    lane = iota((8, 128), 1)
    row = iota((8, 128), 0)
    spread = ((iota((8, 128), 1) % 8) == iota((8, 128), 0)).astype(BF16)
    tiled = dot(routes[...].astype(F32).astype(BF16), spread)
    own = jnp.sum(jnp.where((iota((TITLES, 128), 1) // 8) == iota((TITLES, 128), 0), tiled, 0.0), axis=0, keepdims=True)
    ry[y] = jnp.where(row == y, jnp.broadcast_to(own, (8, 128)), 0.0)

    pl.semaphore_wait(barrier, 1 + (NX - 1) + (NZ - 1) + (NY - 1))

    loop(1, NX, lambda k: a_x(k).start())
    loop(1, NY, lambda k: r_y(k).start())
    loop(1, NZ, lambda k: b_z(k).start())

    def count(first, last):
        def body(step):
            j0 = pl.multiple_of((step // 4) * 64, 64)
            i0 = pl.multiple_of((step % 4) * 256, 256)
            rows = iota((64, 256), 0) + j0
            total = jnp.zeros((64, 256), F32)
            for k in range(FAN):
                total = total + jnp.where(rows == near[k:k + 1, pl.ds(i0, 256)], 1.0, 0.0)
            adj_t[pl.ds(j0, 64), pl.ds(i0, 256)] = total.astype(BF16)
        loop(first, last, body)

    def flip(step):
        r0 = pl.multiple_of((step // 4) * 256, 256)
        c0 = pl.multiple_of((step % 4) * 256, 256)
        adj[pl.ds(r0, 256), pl.ds(c0, 256)] = adj_t[pl.ds(c0, 256), pl.ds(r0, 256)].astype(F32).T.astype(BF16)

    count(0, 12)
    loop(1, NX, lambda k: a_x(k).wait_recv())
    a_z(0, 0).start()
    a_z(0, 1).start()
    a_d(0, 0).start()
    loop(1, NY, lambda k: r_y(k).wait_recv())
    rt[x, c, z] = jnp.sum(ry[...], axis=0)
    loop(1, NZ, lambda k: r_z(k).start())
    count(12, 24)
    loop(1, NZ, lambda k: b_z(k).wait_recv())
    loop(1, NX, lambda k: b_x(k).start())
    b_d(0).start()
    a_z(0, 0).wait_recv()
    a_z(0, 1).wait_recv()
    a_z(1, 0).start()
    a_z(1, 1).start()
    a_d(1, 0).start()
    a_d(1, 1).start()
    loop(1, NZ, lambda k: r_z(k).wait_recv())
    loop(1, NX, lambda k: r_x(k).start())
    r_d(0).start()
    count(24, 40)
    a_z(1, 0).wait_recv()
    a_z(1, 1).wait_recv()
    a_z(2, 0).start()
    a_z(2, 1).start()
    a_d(2, 0).start()
    a_d(2, 1).start()
    loop(1, NX, lambda k: r_x(k).wait_recv())
    loop(1, NX, lambda k: r_d(k).start())
    count(40, 56)
    a_z(2, 0).wait_recv()
    a_z(2, 1).wait_recv()
    a_z(3, 0).start()
    a_z(3, 1).start()
    a_d(3, 0).start()
    a_d(3, 1).start()
    count(56, 64)
    loop(0, 16, flip)
    w_hi[:, :128], w_lo[:, :128] = split(w_self[...])
    w_hi[:, 128:], w_lo[:, 128:] = split(w_neigh[...])

    loop(0, NX, lambda k: r_d(k).wait_recv())
    title = iota((128, 512), 1)
    named = iota((128, 512), 0)
    same = jnp.where((named < 32) & (named // 8 == title % 4), 1.0, 0.0).astype(BF16)
    ahead = jnp.where((named < 32) & (named // 8 < title % 4), 1.0, 0.0).astype(BF16)
    mine = (title // 4) == named
    slot = iota((256, 512), 0)
    col = iota((256, 512), 1)
    match = (
        (slot // 32 == (col % 32) // 4)
        & ((slot % 32) // 4 == (col % 256) // 32)
        & ((slot % 4) // 2 == col // 256)
    )
    wanted = jnp.where(match, (slot % 2).astype(F32) + 1.0, -1.0)

    def select(block):
        listed = rt[block].reshape(128, 128)
        hits = jnp.where(listed == dp.astype(F32), 1.0, 0.0).astype(BF16)
        code = dot(hits, same) * (1.0 + dot(hits, ahead))
        code = jnp.sum(jnp.where(mine, code, 0.0), axis=0, keepdims=True)
        chosen = jnp.where(code == wanted, 1.0, 0.0)
        sel[block] = chosen.astype(BF16)
        sel_t[block] = chosen.T.astype(BF16)

    loop(0, NX, select)

    loop(1, NX, lambda k: b_x(k).wait_recv())
    loop(1, NX, lambda k: b_d(k).start())
    a_z(3, 0).wait_recv()
    a_z(3, 1).wait_recv()
    a_d(4, 0).start()
    a_d(4, 1).start()
    loop(0, NX, lambda k: b_d(k).wait_recv())
    a_d(0, 0).wait_recv()
    for step in range(1, 5):
        a_d(step, 0).wait_recv()
        a_d(step, 1).wait_recv()

    def pack(group):
        gx = group // 4
        gz = (group % 4) * 2
        base = pl.multiple_of(group * 144, 16)
        left = [wa[cc, gz + dz, gx].astype(F32) for dz in range(2) for cc in range(2)]
        right = [wb[cc, gx, gz + dz].astype(F32) for dz in range(2) for cc in range(2)]
        dense[pl.ds(base, 144), :HALF] = jnp.concatenate(left, axis=0).astype(BF16)
        dense[pl.ds(base, 144), HALF:] = jnp.concatenate(right, axis=0).astype(BF16)

    loop(0, 16, pack)

    def project(block):
        rows = dense[pl.ds(pl.multiple_of(block * 256, 256), 256), :]
        qkv[block] = dot(texts[...], rows, NT).astype(BF16).reshape(TITLES, SEQ, 256)

    loop(0, 9, project)

    head = iota((SEQ, 256), 1) // 64

    def attend(step):
        block = step // TITLES
        title_at = step % TITLES
        q = qkv[block, title_at]
        k = qkv[3 + block, title_at]
        v = qkv[6 + block, title_at]
        zero = jnp.zeros_like(k)
        keys = jnp.concatenate([jnp.where(head == h, k, zero) for h in range(4)], axis=0)
        vals = jnp.concatenate([jnp.where(head == h, v, zero) for h in range(4)], axis=0)
        scores = dot(q, keys, NT) * 0.125
        weights = []
        for h in range(4):
            part = scores[:, h * SEQ:(h + 1) * SEQ]
            part = jnp.exp(part - jnp.max(part, axis=1, keepdims=True))
            part = part / jnp.sum(part, axis=1, keepdims=True)
            weights.append(jnp.sum(part.astype(BF16).astype(F32), axis=0, keepdims=True))
        high, low = split(jnp.broadcast_to(jnp.concatenate(weights, axis=1), (8, 512)))
        pooled[step] = (dot(high, vals) + dot(low, vals)) * (1.0 / SEQ)

    loop(0, 3 * TITLES, attend)

    means = jnp.concatenate(
        [
            jnp.concatenate([pooled[b * TITLES + t][0:1] for b in range(3)], axis=1)
            for t in range(TITLES)
        ],
        axis=0,
    )
    center = jnp.mean(means, axis=1, keepdims=True)
    variance = jnp.mean((means - center) ** 2, axis=1, keepdims=True)
    feats[y] = ((means - center) / jnp.sqrt(variance + 1e-05) * gain[...]).astype(BF16)

    loop(1, NY, lambda k: f_y(k).start())
    loop(1, NY, lambda k: f_y(k).wait_recv())
    group_feats = jnp.concatenate([feats[g].astype(F32) for g in range(NY)], axis=0).astype(BF16)
    tg[x, c, z] = (dot(group_feats, w_hi[...]) + dot(group_feats, w_lo[...])).astype(BF16)

    loop(1, NZ, lambda k: t_z(k).start())
    loop(1, NZ, lambda k: t_z(k).wait_recv())
    loop(1, NX, lambda k: t_x(k).start())
    t_d(0).start()

    def place(block):
        rows = dot(sel[block], tg[block].reshape(512, COLS)).astype(BF16)
        for g in range(NY):
            xs[pl.ds(pl.multiple_of(g * 128 + block * 32, 32), 32), :] = rows[g * 32:(g + 1) * 32]

    t_d(0).wait_recv()
    place(x)
    for k in range(1, NX):
        t_x(k).wait_recv()
        t_d(k).start()
    for k in range(1, NX):
        t_d(k).wait_recv()
        place((x - k + NX) % NX)

    def layer(step):
        rows = pl.ds(pl.multiple_of(step * 256, 256), 256)
        total = xs[rows, :128].astype(F32) + dot(adj[rows, :], xs[:, 128:]) + bias[...]
        gate = 1.0 / (1.0 + jnp.exp(-total))
        hidden_out[rows, :] = total * gate
        ds[rows, :128] = (cot[rows, :] * gate * (1.0 + total * (1.0 - gate))).astype(BF16)

    loop(0, 4, layer)

    def backward(step):
        rows = pl.ds(pl.multiple_of(step * 256, 256), 256)
        ds[rows, 128:] = dot(adj_t[rows, :], ds[:, :128]).astype(BF16)

    loop(0, 4, backward)

    def titles_of(block):
        rows = jnp.concatenate(
            [ds[pl.ds(pl.multiple_of(g * 128 + block * 32, 32), 32), :] for g in range(NY)], axis=0
        )
        ub[block] = dot(sel_t[block], rows).astype(BF16).reshape(NC, 256, COLS)

    for k in (1, 2, 3, 0):
        titles_of((x + k) % NX)
        u_d(k).start()
    for k in (1, 2, 3, 0):
        to = (x + k) % NX
        u_d(k).wait_recv()
        vs[to] = (ub[to, c].astype(F32) + ur[to].astype(F32)).astype(BF16)
        if k:
            u_x(k).start()
    total = vs[x].astype(F32)
    for k in range(1, NX):
        u_x(k).wait_recv()
        total = total + vr[k].astype(F32)
    yo[...] = total.astype(BF16).reshape(NZ, 32, COLS)
    loop(1, NZ, lambda k: u_z(k).start())
    node = yo[z].astype(F32)
    for k in range(1, NZ):
        u_z(k).wait_recv()
        node = node + yr[k].astype(F32)
    high, low = split(node)
    partial = dot(high, w_hi[...], NT) + dot(high, w_lo[...], NT) + dot(low, w_hi[...], NT)
    for g in range(NY):
        po[g] = partial[g * 4:(g + 1) * 4].astype(BF16)
    loop(1, NY, lambda k: p_y(k).start())
    result = po[y].astype(F32)
    for k in range(1, NY):
        p_y(k).wait_recv()
        result = result + pr[k].astype(F32)
    grads_out[...] = result

    loop(1, NX, lambda k: a_x(k).wait_send())
    loop(1, NX, lambda k: b_x(k).wait_send())
    loop(1, NX, lambda k: r_x(k).wait_send())
    loop(1, NX, lambda k: t_x(k).wait_send())
    loop(1, NX, lambda k: u_x(k).wait_send())
    loop(1, NZ, lambda k: b_z(k).wait_send())
    loop(1, NZ, lambda k: r_z(k).wait_send())
    loop(1, NZ, lambda k: t_z(k).wait_send())
    loop(1, NZ, lambda k: u_z(k).wait_send())
    loop(1, NY, lambda k: r_y(k).wait_send())
    loop(1, NY, lambda k: f_y(k).wait_send())
    loop(1, NY, lambda k: p_y(k).wait_send())
    loop(0, NX, lambda k: b_d(k).wait_send())
    loop(0, NX, lambda k: r_d(k).wait_send())
    loop(0, NX, lambda k: t_d(k).wait_send())
    loop(0, NX, lambda k: u_d(k).wait_send())
    for step in range(4):
        a_z(step, 0).wait_send()
        a_z(step, 1).wait_send()
    a_d(0, 0).wait_send()
    for step in range(1, 5):
        a_d(step, 0).wait_send()
        a_d(step, 1).wait_send()


def shards(texts, qkv_weight, norm_gain, routes, w_self, w_neigh, gnn_bias, neighbors, cotangent):
    vmem = pl.BlockSpec(memory_space=pltpu.VMEM)
    dma = pltpu.SemaphoreType.DMA
    hidden, grads = pl.pallas_call(
        kernel,
        out_shape=(
            jax.ShapeDtypeStruct((ROWS, 128), F32),
            jax.ShapeDtypeStruct((TITLES, D), F32),
        ),
        in_specs=[vmem] * 9,
        out_specs=(vmem, vmem),
        scratch_shapes=[
            pltpu.VMEM((NC, NZ, NX, 36, HALF), BF16),
            pltpu.VMEM((NC, NX, NZ, 36, HALF), BF16),
            pltpu.VMEM((3 * D, D), BF16),
            pltpu.VMEM((9, TITLES, SEQ, 256), BF16),
            pltpu.VMEM((12, 8, 256), F32),
            pltpu.VMEM((ROWS, ROWS), BF16),
            pltpu.VMEM((ROWS, ROWS), BF16),
            pltpu.VMEM((D, COLS), BF16),
            pltpu.VMEM((D, COLS), BF16),
            pltpu.VMEM((NY, 8, 128), F32),
            pltpu.VMEM((NX, NC, NZ, 8, 128), F32),
            pltpu.VMEM((NX, 256, 512), BF16),
            pltpu.VMEM((NX, 512, 256), BF16),
            pltpu.VMEM((NY, TITLES, D), BF16),
            pltpu.VMEM((NX, NC, NZ, 32, COLS), BF16),
            pltpu.VMEM((ROWS, COLS), BF16),
            pltpu.VMEM((ROWS, COLS), BF16),
            pltpu.VMEM((NX, NC, 256, COLS), BF16),
            pltpu.VMEM((NX, 256, COLS), BF16),
            pltpu.VMEM((NX, 256, COLS), BF16),
            pltpu.VMEM((NX, 256, COLS), BF16),
            pltpu.VMEM((NZ, 32, COLS), BF16),
            pltpu.VMEM((NZ, 32, COLS), BF16),
            pltpu.VMEM((NY, TITLES, D), BF16),
            pltpu.VMEM((NY, TITLES, D), BF16),
            dma((NX,)), dma((NX,)),
            dma((4, 2)), dma((4, 2)),
            dma((5, 2)), dma((5, 2)),
            dma((NZ,)), dma((NZ,)),
            dma((NX,)), dma((NX,)),
            dma((NX,)), dma((NX,)),
            dma((NY,)), dma((NY,)),
            dma((NZ,)), dma((NZ,)),
            dma((NX,)), dma((NX,)),
            dma((NX,)), dma((NX,)),
            dma((NY,)), dma((NY,)),
            dma((NZ,)), dma((NZ,)),
            dma((NX,)), dma((NX,)),
            dma((NX,)), dma((NX,)),
            dma((NX,)), dma((NX,)),
            dma((NX,)), dma((NX,)),
            dma((NZ,)), dma((NZ,)),
            dma((NY,)), dma((NY,)),
        ],
        compiler_params=pltpu.CompilerParams(
            collective_id=0, has_side_effects=True, vmem_limit_bytes=48 * 2**20
        ),
        name="glem_step",
    )(
        texts.reshape(TITLES * SEQ, D),
        qkv_weight.T,
        norm_gain.reshape(1, D),
        routes,
        w_self,
        w_neigh,
        gnn_bias.reshape(1, 128),
        neighbors.T,
        cotangent,
    )
    return hidden, grads


def solution(mesh):
    placed = (
        P(("dp", "graph"), None, None),
        P(None, "dp"),
        P(),
        P(("dp", "graph"), None),
        P(None, "graph"),
        P(None, "graph"),
        P("graph"),
        P("dp", None),
        P("dp", "graph"),
    )
    return jax.shard_map(
        shards,
        mesh=mesh,
        in_specs=placed,
        out_specs=(P("dp", "graph"), P(("dp", "graph"), None)),
        check_vma=False,
    )
```

time: 285 us -> 111 us (0.39)
  waiting for transfers between devices: 181 us -> 0 us
  Pallas kernels: 0 us -> 100 us
  matrix products: 25.7 us -> 0 us
  blocking collectives: 17.4 us -> 0 us
  starting transfers between devices: 13.8 us -> 0 us
  between operations: 14 us -> 0.66 us
  other arithmetic: 13.3 us -> 0 us
  local copies, waits for them, and re-layouts: 18.9 us -> 8.59 us
    all_gather x2 -> x0, waiting for transfers between devices: 117 us -> none  [the longest x1 92.7 us: shards(): lax.all_gather(qkv_weight, 'dp', axis=1, tiled=True)]
    pallas_call x0 -> x1, Pallas kernels: none -> 100 us  [shards(): pl.pallas_call(kernel, out_shape=(jax.ShapeDtypeStruct((ROWS, 128), F32),...]
    reduce_scatter x1 -> x0, waiting for transfers between devices: 49.6 us -> none  [shards(): lax.psum_scatter(jnp.dot(joined, w_both.T, precision=lax.Precision.HIGHES...]
    dot_general x9 -> x0, matrix products: 25.7 us -> none  [the longest x1 7.16 us: shards(): jnp.dot(joined, w_both.T, precision=lax.Precision.HIGHEST, preferred_elem...]
    all_to_all x1 -> x0, blocking collectives: 17.4 us -> none  [shards(): lax.all_to_all(outgoing, 'dp', split_axis=0, concat_axis=0, tiled=True)]
    all_to_all x1 -> x0, starting transfers between devices: 13.7 us -> none  [shards(): lax.all_to_all(own_slab.reshape(part_count, capacity, width), 'dp', split...]
    all_to_all x1 -> x0, waiting for transfers between devices: 13.6 us -> none  [shards(): lax.all_to_all(own_slab.reshape(part_count, capacity, width), 'dp', split...]
    reduce_sum x4 -> x0, other arithmetic: 10 us -> none  [the longest x1 9.54 us: shards(): jnp.sum((neighbors[:, :, None] == row_numbers[None, None, :]).astype(jnp....]
  transfers between devices with their start and end apart: 4 -> 0, of which waited for: 4 -> 0; matrix products, arithmetic and copies ran while one was open for 4% -> 0% of each run, Pallas kernels for 0% -> 0%
where the time goes in v1:
time: 111 us; the launch traced here: 110 us
  Pallas kernels  100 us (90%)
  local copies, waits for them, and re-layouts  8.59 us (8%)
    pallas_call x1, Pallas kernels, shards(): pl.pallas_call(kernel, out_shape=(jax.ShapeDtypeStruct((ROWS, 128), F32),...  100 us
    unnamed x20, local copies, waits for them, and re-layouts  8.59 us

profile of v1, /device:TPU:1, one launch (start us, length us, event | category | flops | bytes accessed | tf_op | source)
XLA Modules:
  0.0 109.6 jit_solution(14849062453475779228)
XLA Ops:
  0.6 0.0 copy-start.8
  0.6 0.7 copy-done.8
  1.3 0.0 copy-start.6
  1.3 0.0 copy-start.7
  1.3 0.7 copy-done.6
  2.0 0.0 copy-done.7
  2.0 0.0 copy-start
  2.0 1.1 %copy-done = bf16[4,128,768]{2,1,0:T(8,128)(2,1)S(1)} copy-done((bf16[4,128,768]{2,1,0:T(8,128)(2,1)S(1)}, bf16[4,128,768]{2,1,0:T(8,128)(2,1)}, u32[]{:S(2)}) %copy-start) | copy-done | bytes 786456
  3.1 0.0 copy-start.1
  3.1 1.0 copy-done.1
  4.2 0.0 copy-start.2
  4.2 1.0 copy-done.2
  5.2 0.0 copy-start.3
  5.2 1.0 copy-done.3
  6.2 0.0 copy-start.4
  6.2 0.8 copy-done.4
  7.0 0.0 copy-start.5
  7.0 0.8 copy-done.5
  7.8 100.4 %glem_step.1 = (f32[1024,128]{1,0:T(8,128)S(1)}, f32[4,768]{1,0:T(4,128)S(1)}) custom-call(bf16[512,768]{1,0:T(8,128)(2,1)S(1)} %bitcast.4, bf16[36,768]{1,0:T(8,128)(2,1)S(1)} %bitcast.6, f32[1,768]{1,0:T(1,128)S(1)} %reshape.14.gain, s32[4,8]{1,0:T(4,128)S(1)} %copy-done.6, f32[768,128]{1,0:T(8,128)S(1)} %copy-done.2, f32[768,128]{1,0:T(8,128)S(1)} %copy-done.3, ...), custom_call_target="tpu_custom_call" | custom-call | tf_op jit(solution)/shard_map/glem_step/pallas_call | solution.py:424
  108.2 0.8 copy.13
  109.0 0.6 copy.14
  (1 shorter events, 0.0 us)
Async XLA Ops:
  0.6 0.7 copy-start.8
  1.3 0.7 copy-start.6
  1.3 0.7 copy-start.7
  2.0 1.1 %copy-start = (bf16[4,128,768]{2,1,0:T(8,128)(2,1)S(1)}, bf16[4,128,768]{2,1,0:T(8,128)(2,1)}, u32[]{:S(2)}) copy-start(bf16[4,128,768]{2,1,0:T(8,128)(2,1)} %param.9) | copy-start | bytes 2359300
  3.1 1.0 copy-start.1
  4.2 1.0 copy-start.2
  5.2 1.0 copy-start.3
  6.2 0.8 copy-start.4
  7.0 0.8 copy-start.5

commit v2 on v1

v2 whole, which is shorter than its diff:
```python
import functools

import jax
import jax.numpy as jnp
from jax import lax
from jax.experimental import pallas as pl
from jax.experimental.pallas import tpu as pltpu
from jax.sharding import PartitionSpec as P

NX, NZ, NC, NY = 4, 8, 2, 8
D = 768
HALF = 384
WIDE = 36
PIECE = 112
TITLES = 4
SEQ = 128
COLS = 256
ROWS = 1024
FAN = 15
BF16 = jnp.bfloat16
F32 = jnp.float32
NT = (((1,), (1,)), ((), ()))
NN = (((1,), (0,)), ((), ()))


def dot(a, b, dims=NN):
    return lax.dot_general(a, b, dims, preferred_element_type=F32)


def split(value):
    high = value.astype(BF16)
    return high, (value - high.astype(F32)).astype(BF16)


def iota(shape, axis):
    return lax.broadcasted_iota(jnp.int32, shape, axis)


def kernel(
    texts_in, wt_in, gain_in, routes_in, w_self_in, w_neigh_in, bias_in, near_in, cot_in,
    hidden_out, grads_out,
    texts, wt, gain, routes, w_self, w_neigh, bias, near, cot, load,
    wa, wb, dense, qt, keys, vals, pooled, adj_t, adj, w_hi, w_lo,
    ry, rt, sel, sel_t, feats, tg, xs, ds, ub, ur, vs, vr, yo, yr, po, pr,
    sa_x, ra_x, sa_z, ra_z, sa_d, ra_d, sb_z, rb_z, sb_x, rb_x, sb_d, rb_d,
    sr_y, rr_y, sr_z, rr_z, sr_x, rr_x, sr_d, rr_d,
    sf, rf, st_z, rt_z, st_x, rt_x, st_d, rt_d,
    su_d, ru_d, su_x, ru_x, su_z, ru_z, sp, rp,
):
    dp = lax.axis_index("dp")
    y = lax.axis_index("graph")
    x = dp // 16
    z = (dp // 2) % 8
    c = dp % 2
    other = 1 - c

    def at(px, pz, pc, py):
        return (px * 16 + pz * 2 + pc, py)

    def xp(k):
        return at((x + k) % NX, z, c, y)

    def zp(k):
        return at(x, (z + k) % NZ, c, y)

    def yp(k):
        return at(x, z, c, (y + k) % NY)

    mate = at(x, z, other, y)

    def send(src, dst, ssem, rsem, peer):
        return pltpu.make_async_remote_copy(
            src_ref=src, dst_ref=dst, send_sem=ssem, recv_sem=rsem,
            device_id=peer, device_id_type=pl.DeviceIdType.MESH,
        )

    def loop(low, high, body):
        def step(i, carry):
            body(i)
            return carry
        lax.fori_loop(low, high, step, 0)

    barrier = pltpu.get_barrier_semaphore()

    def greet(peer):
        pl.semaphore_signal(barrier, inc=1, device_id=peer, device_id_type=pl.DeviceIdType.MESH)

    greet(mate)
    loop(1, NX, lambda k: greet(xp(k)))
    loop(1, NZ, lambda k: greet(zp(k)))
    loop(1, NY, lambda k: greet(yp(k)))

    held = (texts, wt, gain, routes, w_self, w_neigh, bias, near, cot)
    given = (texts_in, wt_in, gain_in, routes_in, w_self_in, w_neigh_in, bias_in, near_in, cot_in)
    loads = [pltpu.make_async_copy(given[i], held[i], load.at[i]) for i in range(9)]
    for i in (1, 3, 7, 4, 5, 0, 2, 6, 8):
        loads[i].start()

    def a_x(k):
        return send(wa.at[c, z, x], wa.at[c, z, x], sa_x.at[k], ra_x.at[k], xp(k))

    def ring(step, way, sub):
        hops = step if way == 0 else -step
        return wa.at[c, (z - hops + NZ) % NZ, pl.ds(2 * sub, 2)]

    def a_z(step, way, sub):
        part = ring(step, way, sub)
        peer = zp(1) if way == 0 else zp(NZ - 1)
        return send(part, part, sa_z.at[step, way, sub], ra_z.at[step, way, sub], peer)

    def a_d(step, way, sub):
        part = ring(step, way, sub)
        return send(part, part, sa_d.at[step, way, sub], ra_d.at[step, way, sub], mate)

    def b_z(k):
        return send(wb.at[c, x, z], wb.at[c, x, z], sb_z.at[k], rb_z.at[k], zp(k))

    def b_x(k):
        return send(wb.at[c, x], wb.at[c, x], sb_x.at[k], rb_x.at[k], xp(k))

    def b_s(k, dz):
        part = wb.at[c, x, (z + dz) % NZ]
        return send(part, part, sb_x.at[k], rb_x.at[k], xp(k))

    def b_d(k):
        part = wb.at[c, (x - k + NX) % NX]
        return send(part, part, sb_d.at[k], rb_d.at[k], mate)

    def r_y(k):
        return send(ry.at[y], ry.at[y], sr_y.at[k], rr_y.at[k], yp(k))

    def r_z(k):
        return send(rt.at[x, c, z], rt.at[x, c, z], sr_z.at[k], rr_z.at[k], zp(k))

    def r_x(k):
        return send(rt.at[x, c], rt.at[x, c], sr_x.at[k], rr_x.at[k], xp(k))

    def r_d(k):
        part = rt.at[(x - k + NX) % NX, c]
        return send(part, part, sr_d.at[k], rr_d.at[k], mate)

    def f_y(k):
        return send(feats.at[y], feats.at[y], sf.at[k], rf.at[k], yp(k))

    def t_z(k):
        return send(tg.at[x, c, z], tg.at[x, c, z], st_z.at[k], rt_z.at[k], zp(k))

    def t_x(k):
        return send(tg.at[x, c], tg.at[x, c], st_x.at[k], rt_x.at[k], xp(k))

    def t_s(k, dz):
        part = tg.at[x, c, (z + dz) % NZ]
        return send(part, part, st_x.at[k], rt_x.at[k], xp(k))

    def t_d(k):
        part = tg.at[(x - k + NX) % NX, c]
        return send(part, part, st_d.at[k], rt_d.at[k], mate)

    def u_d(k):
        to = (x + k) % NX
        return send(ub.at[to, other], ur.at[to], su_d.at[k], ru_d.at[k], mate)

    def u_x(k, dz):
        to = (z + dz) % NZ
        return send(vs.at[(x + k) % NX, to], vr.at[k, dz], su_x.at[k, dz], ru_x.at[k, dz], xp(k))

    def u_z(k):
        return send(yo.at[k], yr.at[k], su_z.at[k], ru_z.at[k], zp(k))

    def p_y(k):
        return send(po.at[(y + k) % NY], pr.at[k], sp.at[k], rp.at[k], yp(k))

    loads[1].wait()
    shard = wt[...].astype(F32)
    filling = jnp.zeros((PIECE - 3 * WIDE, 128), F32)
    tiles = [shard[:, i * 128:(i + 1) * 128] for i in range(6)]
    wa[c, z, x] = jnp.concatenate(tiles[:3] + [filling], axis=0).astype(BF16)
    wb[c, x, z] = jnp.concatenate(tiles[3:] + [filling], axis=0).astype(BF16)
    loads[3].wait()
    row = iota((8, 128), 0)
    spread = ((iota((8, 128), 1) % 8) == iota((8, 128), 0)).astype(BF16)
    tiled = dot(routes[...].astype(F32).astype(BF16), spread)
    own = jnp.sum(jnp.where((iota((TITLES, 128), 1) // 8) == iota((TITLES, 128), 0), tiled, 0.0), axis=0, keepdims=True)
    ry[y] = jnp.where(row == y, jnp.broadcast_to(own, (8, 128)), 0.0)

    pl.semaphore_wait(barrier, 1 + (NX - 1) + (NZ - 1) + (NY - 1))

    loop(1, NX, lambda k: a_x(k).start())
    for k in (1, 7, 2, 6, 3, 5, 4):
        b_z(k).start()
    loop(1, NX, lambda k: b_s(k, 0).start())
    loop(1, NY, lambda k: r_y(k).start())

    def count(first, last):
        def body(step):
            j0 = pl.multiple_of((step // 4) * 64, 64)
            i0 = pl.multiple_of((step % 4) * 256, 256)
            rows = iota((64, 256), 0) + j0
            total = jnp.zeros((64, 256), F32)
            for k in range(FAN):
                total = total + jnp.where(rows == near[k:k + 1, pl.ds(i0, 256)], 1.0, 0.0)
            adj_t[pl.ds(j0, 64), pl.ds(i0, 256)] = total.astype(BF16)
        loop(first, last, body)

    def flip(step):
        r0 = pl.multiple_of((step // 4) * 256, 256)
        c0 = pl.multiple_of((step % 4) * 256, 256)
        adj[pl.ds(r0, 256), pl.ds(c0, 256)] = adj_t[pl.ds(c0, 256), pl.ds(r0, 256)].astype(F32).T.astype(BF16)

    def pass_b(k):
        b_z(k).wait_recv()
        loop(1, NX, lambda n: b_s(n, NZ - k).start())

    def pass_a(step):
        for way in range(2):
            for sub in range(2):
                a_z(step, way, sub).wait_recv()
                if step < 2 or way == sub:
                    a_z(step + 1, way, sub).start()
                a_d(step + 1, way, sub).start()

    loads[7].wait()
    count(0, 24)
    loop(1, NX, lambda k: a_x(k).wait_recv())
    for sub in range(2):
        for way in range(2):
            a_z(0, way, sub).start()
    a_d(0, 0, 0).start()
    a_d(0, 0, 1).start()
    pass_b(1)
    pass_b(7)
    count(24, 32)
    pass_b(2)
    pass_b(6)
    loop(1, NY, lambda k: r_y(k).wait_recv())
    rt[x, c, z] = jnp.sum(ry[...], axis=0)
    loop(1, NZ, lambda k: r_z(k).start())
    pass_a(0)
    pass_b(3)
    pass_b(5)
    pass_b(4)
    b_d(0).start()
    count(32, 44)
    pass_a(1)
    loop(1, NZ, lambda k: r_z(k).wait_recv())
    loop(1, NX, lambda k: r_x(k).start())
    r_d(0).start()
    count(44, 56)
    pass_a(2)
    loop(1, NX, lambda k: r_x(k).wait_recv())
    loop(1, NX, lambda k: r_d(k).start())
    count(56, 64)
    loads[4].wait()
    loads[5].wait()
    w_hi[:, :128], w_lo[:, :128] = split(w_self[...])
    w_hi[:, 128:], w_lo[:, 128:] = split(w_neigh[...])

    for k in (1, 3, 2):
        b_x(k).wait_recv()
        b_d(k).start()
    a_z(3, 0, 0).wait_recv()
    a_d(4, 0, 0).start()
    a_z(3, 1, 1).wait_recv()
    a_d(4, 1, 1).start()
    a_d(0, 0, 0).wait_recv()
    a_d(0, 0, 1).wait_recv()
    for step in range(1, 4):
        for way in range(2):
            for sub in range(2):
                a_d(step, way, sub).wait_recv()
    loop(0, NX, lambda k: b_d(k).wait_recv())
    a_d(4, 0, 0).wait_recv()
    a_d(4, 1, 1).wait_recv()
    loads[0].wait()
    loads[2].wait()
    loads[6].wait()
    loads[8].wait()

    def pack(group):
        gx = group // 4
        gz = (group % 4) * 2
        base = pl.multiple_of(group * 144, 16)
        left = [wa[cc, gz + dz, gx].astype(F32) for dz in range(2) for cc in range(2)]
        right = [wb[cc, gx, gz + dz].astype(F32) for dz in range(2) for cc in range(2)]
        for i in range(3):
            rows = slice(i * WIDE, (i + 1) * WIDE)
            for start, pieces in ((0, left), (HALF, right)):
                column = jnp.concatenate([piece[rows] for piece in pieces], axis=0)
                dense[pl.ds(base, 144), start + i * 128:start + (i + 1) * 128] = column.astype(BF16)

    loop(0, 16, pack)

    def project(block):
        at0 = pl.multiple_of(block * 256, 256)
        rows = pl.ds(at0, 256)
        title_q = dot(dense[rows, :], texts[...], NT).astype(BF16)
        for t in range(TITLES):
            qt[block, t] = title_q[:, t * SEQ:(t + 1) * SEQ]
        rows = pl.ds(pl.multiple_of(at0 + D, 256), 256)
        keys[block] = dot(texts[...], dense[rows, :], NT).astype(BF16).reshape(TITLES, SEQ, 256)
        rows = pl.ds(pl.multiple_of(at0 + 2 * D, 256), 256)
        vals[block] = dot(texts[...], dense[rows, :], NT).astype(BF16).reshape(TITLES, SEQ, 256)

    loop(0, 3, project)

    adder = jnp.where((iota((8, 4 * SEQ), 1) // SEQ) == (iota((8, 4 * SEQ), 0) % 4), 1.0, 0.0).astype(BF16)
    upper = iota((8, SEQ), 0) < 4
    own_head = (iota((8, 256), 1) // 64) == (iota((8, 256), 0) % 4)
    blank = jnp.zeros((64, SEQ), BF16)

    def attend(block):
        each = range(TITLES)
        scores = []
        for t in each:
            q = qt[block, t]
            queries = jnp.concatenate(
                [
                    jnp.concatenate([q[h * 64:(h + 1) * 64] if i == h else blank for i in range(4)], axis=1)
                    for h in range(4)
                ],
                axis=0,
            )
            scores.append(dot(keys[block, t], queries) * 0.125)
        scores = [jnp.exp(s - jnp.max(s, axis=0, keepdims=True)) for s in scores]
        probs = [(s * (1.0 / jnp.sum(s, axis=0, keepdims=True))).astype(BF16) for s in scores]
        sums = [split(dot(adder, p, NT)) for p in probs]
        sums = [jnp.where(upper, high.astype(F32), low.astype(F32)).astype(BF16) for high, low in sums]
        mixed = [dot(sums[t], vals[block, t]) for t in each]
        for t in each:
            row = jnp.sum(jnp.where(own_head, mixed[t], 0.0), axis=0, keepdims=True) * (1.0 / SEQ)
            pooled[block * TITLES + t] = jnp.broadcast_to(row, (8, 256))

    loop(0, 3, attend)

    means = jnp.concatenate(
        [
            jnp.concatenate([pooled[b * TITLES + t][0:1] for b in range(3)], axis=1)
            for t in range(TITLES)
        ],
        axis=0,
    )
    center = jnp.mean(means, axis=1, keepdims=True)
    variance = jnp.mean((means - center) ** 2, axis=1, keepdims=True)
    feats[y] = ((means - center) / jnp.sqrt(variance + 1e-05) * gain[...]).astype(BF16)

    loop(1, NY, lambda k: f_y(k).start())
    loop(0, NX, lambda k: r_d(k).wait_recv())
    title = iota((128, 512), 1)
    named = iota((128, 512), 0)
    same = jnp.where((named < 32) & (named // 8 == title % 4), 1.0, 0.0).astype(BF16)
    ahead = jnp.where((named < 32) & (named // 8 < title % 4), 1.0, 0.0).astype(BF16)
    mine = (title // 4) == named
    slot = iota((256, 512), 0)
    col = iota((256, 512), 1)
    match = (
        (slot // 32 == (col % 32) // 4)
        & ((slot % 32) // 4 == (col % 256) // 32)
        & ((slot % 4) // 2 == col // 256)
    )
    wanted = jnp.where(match, (slot % 2).astype(F32) + 1.0, -1.0)

    def select(block):
        listed = rt[block].reshape(128, 128)
        hits = jnp.where(listed == dp.astype(F32), 1.0, 0.0).astype(BF16)
        code = dot(hits, same) * (1.0 + dot(hits, ahead))
        code = jnp.sum(jnp.where(mine, code, 0.0), axis=0, keepdims=True)
        chosen = jnp.where(code == wanted, 1.0, 0.0)
        sel[block] = chosen.astype(BF16)
        sel_t[block] = chosen.T.astype(BF16)

    loop(0, NX, select)

    loop(1, NY, lambda k: f_y(k).wait_recv())
    group_feats = jnp.concatenate([feats[g].astype(F32) for g in range(NY)], axis=0).astype(BF16)
    tg[x, c, z] = (dot(group_feats, w_hi[...]) + dot(group_feats, w_lo[...])).astype(BF16)

    for k in (1, 7, 2, 6, 3, 5, 4):
        t_z(k).start()
    loop(1, NX, lambda k: t_s(k, 0).start())
    loop(0, 16, flip)
    for k in (1, 7, 2, 6, 3, 5, 4):
        t_z(k).wait_recv()
        loop(1, NX, lambda n: t_s(n, NZ - k).start())
    t_d(0).start()

    def place(block):
        rows = dot(sel[block], tg[block].reshape(512, COLS)).astype(BF16)
        for g in range(NY):
            xs[pl.ds(pl.multiple_of(g * 128 + block * 32, 32), 32), :] = rows[g * 32:(g + 1) * 32]

    t_d(0).wait_recv()
    place(x)
    for k in (1, 3, 2):
        t_x(k).wait_recv()
        t_d(k).start()
    for k in (1, 3, 2):
        t_d(k).wait_recv()
        place((x - k + NX) % NX)

    def layer(step):
        rows = pl.ds(pl.multiple_of(step * 256, 256), 256)
        total = xs[rows, :128].astype(F32) + dot(adj[rows, :], xs[:, 128:]) + bias[...]
        gate = 1.0 / (1.0 + jnp.exp(-total))
        hidden_out[rows, :] = total * gate
        ds[rows, :128] = (cot[rows, :] * gate * (1.0 + total * (1.0 - gate))).astype(BF16)

    loop(0, 4, layer)

    def backward(step):
        rows = pl.ds(pl.multiple_of(step * 256, 256), 256)
        ds[rows, 128:] = dot(adj_t[rows, :], ds[:, :128]).astype(BF16)

    loop(0, 4, backward)

    def titles_of(block):
        rows = jnp.concatenate(
            [ds[pl.ds(pl.multiple_of(g * 128 + block * 32, 32), 32), :] for g in range(NY)], axis=0
        )
        ub[block] = dot(sel_t[block], rows).astype(BF16).reshape(NC, 256, COLS)

    for k in (1, 2, 3, 0):
        titles_of((x + k) % NX)
        u_d(k).start()
    for k in (1, 2, 3):
        to = (x + k) % NX
        u_d(k).wait_recv()
        vs[to] = (ub[to, c].astype(F32) + ur[to].astype(F32)).astype(BF16).reshape(NZ, 32, COLS)
        loop(0, NZ, lambda dz: u_x(k, (dz + 4) % NZ).start())
    u_d(0).wait_recv()
    vs[x] = (ub[x, c].astype(F32) + ur[x].astype(F32)).astype(BF16).reshape(NZ, 32, COLS)

    def gathered(dz):
        total = vs[x, (z + dz) % NZ].astype(F32)
        for k in (1, 3, 2):
            u_x(k, dz).wait_recv()
            total = total + vr[k, dz].astype(F32)
        return total

    for dz in (4, 5, 3, 6, 2, 7, 1):
        yo[dz] = gathered(dz).astype(BF16)
        u_z(dz).start()
    node = gathered(0)
    for k in (1, 7, 2, 6, 3, 5, 4):
        u_z(k).wait_recv()
        node = node + yr[k].astype(F32)
    high, low = split(node)
    partial = dot(high, w_hi[...], NT) + dot(high, w_lo[...], NT) + dot(low, w_hi[...], NT)
    for g in range(NY):
        po[g] = partial[g * 4:(g + 1) * 4].astype(BF16)
    loop(1, NY, lambda k: p_y(k).start())
    result = po[y].astype(F32)
    for k in range(1, NY):
        p_y(k).wait_recv()
        result = result + pr[k].astype(F32)
    grads_out[...] = result

    loop(1, NX, lambda k: a_x(k).wait_send())
    loop(1, NX, lambda k: b_x(k).wait_send())
    loop(1, NX, lambda k: r_x(k).wait_send())
    loop(1, NX, lambda k: t_x(k).wait_send())
    for k in range(1, NX):
        loop(0, NZ, lambda dz: u_x(k, dz).wait_send())
    loop(1, NZ, lambda k: b_z(k).wait_send())
    loop(1, NZ, lambda k: r_z(k).wait_send())
    loop(1, NZ, lambda k: t_z(k).wait_send())
    loop(1, NZ, lambda k: u_z(k).wait_send())
    loop(1, NY, lambda k: r_y(k).wait_send())
    loop(1, NY, lambda k: f_y(k).wait_send())
    loop(1, NY, lambda k: p_y(k).wait_send())
    loop(0, NX, lambda k: b_d(k).wait_send())
    loop(0, NX, lambda k: r_d(k).wait_send())
    loop(0, NX, lambda k: t_d(k).wait_send())
    loop(0, NX, lambda k: u_d(k).wait_send())
    for step in range(4):
        for way in range(2):
            for sub in range(2):
                if step < 3 or way == sub:
                    a_z(step, way, sub).wait_send()
    a_d(0, 0, 0).wait_send()
    a_d(0, 0, 1).wait_send()
    for step in range(1, 5):
        for way in range(2):
            for sub in range(2):
                if step < 4 or way == sub:
                    a_d(step, way, sub).wait_send()


def shards(texts, qkv_weight, norm_gain, routes, w_self, w_neigh, gnn_bias, neighbors, cotangent):
    vmem = pl.BlockSpec(memory_space=pltpu.VMEM)
    dma = pltpu.SemaphoreType.DMA
    hidden, grads = pl.pallas_call(
        kernel,
        out_shape=(
            jax.ShapeDtypeStruct((ROWS, 128), F32),
            jax.ShapeDtypeStruct((TITLES, D), F32),
        ),
        in_specs=[pl.BlockSpec(memory_space=pl.ANY)] * 9,
        out_specs=(vmem, vmem),
        scratch_shapes=[
            pltpu.VMEM((TITLES * SEQ, D), BF16),
            pltpu.VMEM((36, D), BF16),
            pltpu.VMEM((1, D), F32),
            pltpu.VMEM((TITLES, 8), jnp.int32),
            pltpu.VMEM((D, 128), F32),
            pltpu.VMEM((D, 128), F32),
            pltpu.VMEM((1, 128), F32),
            pltpu.VMEM((FAN, ROWS), jnp.int32),
            pltpu.VMEM((ROWS, 128), F32),
            dma((9,)),
            pltpu.VMEM((NC, NZ, NX, PIECE, 128), BF16),
            pltpu.VMEM((NC, NX, NZ, PIECE, 128), BF16),
            pltpu.VMEM((3 * D, D), BF16),
            pltpu.VMEM((3, TITLES, 256, SEQ), BF16),
            pltpu.VMEM((3, TITLES, SEQ, 256), BF16),
            pltpu.VMEM((3, TITLES, SEQ, 256), BF16),
            pltpu.VMEM((12, 8, 256), F32),
            pltpu.VMEM((ROWS, ROWS), BF16),
            pltpu.VMEM((ROWS, ROWS), BF16),
            pltpu.VMEM((D, COLS), BF16),
            pltpu.VMEM((D, COLS), BF16),
            pltpu.VMEM((NY, 8, 128), F32),
            pltpu.VMEM((NX, NC, NZ, 8, 128), F32),
            pltpu.VMEM((NX, 256, 512), BF16),
            pltpu.VMEM((NX, 512, 256), BF16),
            pltpu.VMEM((NY, TITLES, D), BF16),
            pltpu.VMEM((NX, NC, NZ, 32, COLS), BF16),
            pltpu.VMEM((ROWS, COLS), BF16),
            pltpu.VMEM((ROWS, COLS), BF16),
            pltpu.VMEM((NX, NC, 256, COLS), BF16),
            pltpu.VMEM((NX, 256, COLS), BF16),
            pltpu.VMEM((NX, NZ, 32, COLS), BF16),
            pltpu.VMEM((NX, NZ, 32, COLS), BF16),
            pltpu.VMEM((NZ, 32, COLS), BF16),
            pltpu.VMEM((NZ, 32, COLS), BF16),
            pltpu.VMEM((NY, TITLES, D), BF16),
            pltpu.VMEM((NY, TITLES, D), BF16),
            dma((NX,)), dma((NX,)),
            dma((4, 2, 2)), dma((4, 2, 2)),
            dma((5, 2, 2)), dma((5, 2, 2)),
            dma((NZ,)), dma((NZ,)),
            dma((NX,)), dma((NX,)),
            dma((NX,)), dma((NX,)),
            dma((NY,)), dma((NY,)),
            dma((NZ,)), dma((NZ,)),
            dma((NX,)), dma((NX,)),
            dma((NX,)), dma((NX,)),
            dma((NY,)), dma((NY,)),
            dma((NZ,)), dma((NZ,)),
            dma((NX,)), dma((NX,)),
            dma((NX,)), dma((NX,)),
            dma((NX,)), dma((NX,)),
            dma((NX, NZ)), dma((NX, NZ)),
            dma((NZ,)), dma((NZ,)),
            dma((NY,)), dma((NY,)),
        ],
        compiler_params=pltpu.CompilerParams(
            collective_id=0, has_side_effects=True, vmem_limit_bytes=60 * 2**20
        ),
        name="glem_step",
    )(
        texts.reshape(TITLES * SEQ, D),
        qkv_weight.T,
        norm_gain.reshape(1, D),
        routes,
        w_self,
        w_neigh,
        gnn_bias.reshape(1, 128),
        neighbors.T,
        cotangent,
    )
    return hidden, grads


def solution(mesh):
    placed = (
        P(("dp", "graph"), None, None),
        P(None, "dp"),
        P(),
        P(("dp", "graph"), None),
        P(None, "graph"),
        P(None, "graph"),
        P("graph"),
        P("dp", None),
        P("dp", "graph"),
    )
    return jax.shard_map(
        shards,
        mesh=mesh,
        in_specs=placed,
        out_specs=(P("dp", "graph"), P(("dp", "graph"), None)),
        check_vma=False,
    )
```

time: 111 us -> 89.8 us (0.81)
  Pallas kernels: 100 us -> 85 us
  local copies, waits for them, and re-layouts: 8.59 us -> 3.74 us
    pallas_call x1, Pallas kernels: 100 us -> 85 us  [shards(): pl.pallas_call(kernel, out_shape=(jax.ShapeDtypeStruct((ROWS, 128), F32),...]
    unnamed x20 -> x6, local copies, waits for them, and re-layouts: 8.59 us -> 3.16 us
where the time goes in v2:
time: 89.8 us; the launch traced here: 89.4 us
  Pallas kernels  85 us (95%)
  local copies, waits for them, and re-layouts  3.74 us (4%)
    pallas_call x1, Pallas kernels, shards(): pl.pallas_call(kernel, out_shape=(jax.ShapeDtypeStruct((ROWS, 128), F32),...  85 us
    unnamed x6, local copies, waits for them, and re-layouts  3.16 us

profile of v2, /device:TPU:1, one launch (start us, length us, event | category | flops | bytes accessed | tf_op | source)
XLA Modules:
  0.0 89.4 jit_solution(4120712785044592536)
XLA Ops:
  0.6 0.0 copy-start.1
  0.6 0.7 copy-done.1
  1.3 0.6 reshape.14.gain_in
  1.9 85.0 %glem_step.1 = (f32[1024,128]{1,0:T(8,128)}, f32[4,768]{1,0:T(4,128)}) custom-call(bf16[512,768]{1,0:T(8,128)(2,1)} %bitcast.4, bf16[36,768]{1,0:T(8,128)(2,1)} %bitcast.6, f32[1,768]{1,0:T(1,128)} %reshape.14.gain_in, s32[4,8]{1,0:T(4,128)} %routes_in.1, f32[768,128]{1,0:T(8,128)} %w_self_in.1, f32[768,128]{1,0:T(8,128)} %w_neigh_in.1, f32[1,128]{1,0:T(1,128)} %bitcast.7, ...), custom_call_target="tpu_custom_call" | custom-call | tf_op jit(solution)/shard_map/glem_step/pallas_call | solution.py:491
  86.9 0.0 copy-start
  86.9 1.9 %copy.13 = f32[1024,128]{1,0:T(8,128)} copy(f32[1024,128]{1,0:T(8,128)} %get-tuple-element.4) | data formatting | bytes 1048576
  88.8 0.0 copy-done
  88.8 0.6 copy.14
Async XLA Ops:
  0.6 0.7 copy-start.1
  86.9 1.9 %copy-start = (f32[4,768]{1,0:T(4,128)S(1)}, f32[4,768]{1,0:T(4,128)}, u32[]{:S(2)}) copy-start(f32[4,768]{1,0:T(4,128)} %get-tuple-element.5) | copy-start | bytes 36868

commit v3 on v2

--- a/solution.py
+++ b/solution.py
@@ -9,9 +9,9 @@
 
 NX, NZ, NC, NY = 4, 8, 2, 8
 D = 768
-HALF = 384
 WIDE = 36
-PIECE = 112
+PIECE_A = 80
+PIECE_B = 144
 TITLES = 4
 SEQ = 128
 COLS = 256
@@ -85,10 +85,12 @@
     def greet(peer):
         pl.semaphore_signal(barrier, inc=1, device_id=peer, device_id_type=pl.DeviceIdType.MESH)
 
+    for k in (4, 3, 5, 2, 6, 1, 7):
+        greet(zp(k))
+        greet(yp(k))
+    for k in (2, 1, 3):
+        greet(xp(k))
     greet(mate)
-    loop(1, NX, lambda k: greet(xp(k)))
-    loop(1, NZ, lambda k: greet(zp(k)))
-    loop(1, NY, lambda k: greet(yp(k)))
 
     held = (texts, wt, gain, routes, w_self, w_neigh, bias, near, cot)
     given = (texts_in, wt_in, gain_in, routes_in, w_self_in, w_neigh_in, bias_in, near_in, cot_in)
@@ -108,9 +110,12 @@
         peer = zp(1) if way == 0 else zp(NZ - 1)
         return send(part, part, sa_z.at[step, way, sub], ra_z.at[step, way, sub], peer)
 
-    def a_d(step, way, sub):
-        part = ring(step, way, sub)
-        return send(part, part, sa_d.at[step, way, sub], ra_d.at[step, way, sub], mate)
+    def a_d(step, way):
+        if step == 4:
+            part = ring(step, way, way)
+        else:
+            part = wa.at[c, (z - (step if way == 0 else -step) + NZ) % NZ]
+        return send(part, part, sa_d.at[step, way], ra_d.at[step, way], mate)
 
     def b_z(k):
         return send(wb.at[c, x, z], wb.at[c, x, z], sb_z.at[k], rb_z.at[k], zp(k))
@@ -172,10 +177,10 @@
 
     loads[1].wait()
     shard = wt[...].astype(F32)
-    filling = jnp.zeros((PIECE - 3 * WIDE, 128), F32)
+    filling = jnp.zeros((PIECE_A - 2 * WIDE, 128), F32)
     tiles = [shard[:, i * 128:(i + 1) * 128] for i in range(6)]
-    wa[c, z, x] = jnp.concatenate(tiles[:3] + [filling], axis=0).astype(BF16)
-    wb[c, x, z] = jnp.concatenate(tiles[3:] + [filling], axis=0).astype(BF16)
+    wa[c, z, x] = jnp.concatenate(tiles[:2] + [filling], axis=0).astype(BF16)
+    wb[c, x, z] = jnp.concatenate(tiles[2:], axis=0).astype(BF16)
     loads[3].wait()
     row = iota((8, 128), 0)
     spread = ((iota((8, 128), 1) % 8) == iota((8, 128), 0)).astype(BF16)
@@ -188,7 +193,8 @@
     loop(1, NX, lambda k: a_x(k).start())
     for k in (1, 7, 2, 6, 3, 5, 4):
         b_z(k).start()
-    loop(1, NX, lambda k: b_s(k, 0).start())
+    for k in range(1, NX):
+        b_s(k, 0).start()
     loop(1, NY, lambda k: r_y(k).start())
 
     def count(first, last):
@@ -209,15 +215,17 @@
 
     def pass_b(k):
         b_z(k).wait_recv()
-        loop(1, NX, lambda n: b_s(n, NZ - k).start())
+        for n in range(1, NX):
+            b_s(n, NZ - k).start()
 
     def pass_a(step):
-        for way in range(2):
-            for sub in range(2):
+        for sub in range(2):
+            for way in range(2):
                 a_z(step, way, sub).wait_recv()
                 if step < 2 or way == sub:
                     a_z(step + 1, way, sub).start()
-                a_d(step + 1, way, sub).start()
+        for way in range(2):
+            a_d(step + 1, way).start()
 
     loads[7].wait()
     count(0, 24)
@@ -225,56 +233,46 @@
     for sub in range(2):
         for way in range(2):
             a_z(0, way, sub).start()
-    a_d(0, 0, 0).start()
-    a_d(0, 0, 1).start()
+    a_d(0, 0).start()
     pass_b(1)
     pass_b(7)
     count(24, 32)
     pass_b(2)
     pass_b(6)
-    loop(1, NY, lambda k: r_y(k).wait_recv())
-    rt[x, c, z] = jnp.sum(ry[...], axis=0)
-    loop(1, NZ, lambda k: r_z(k).start())
     pass_a(0)
     pass_b(3)
     pass_b(5)
     pass_b(4)
     b_d(0).start()
-    count(32, 44)
+    count(32, 38)
     pass_a(1)
-    loop(1, NZ, lambda k: r_z(k).wait_recv())
-    loop(1, NX, lambda k: r_x(k).start())
-    r_d(0).start()
-    count(44, 56)
+    loop(1, NY, lambda k: r_y(k).wait_recv())
+    rt[x, c, z] = jnp.sum(ry[...], axis=0)
+    loop(1, NZ, lambda k: r_z(k).start())
     pass_a(2)
-    loop(1, NX, lambda k: r_x(k).wait_recv())
-    loop(1, NX, lambda k: r_d(k).start())
-    count(56, 64)
-    loads[4].wait()
-    loads[5].wait()
-    w_hi[:, :128], w_lo[:, :128] = split(w_self[...])
-    w_hi[:, 128:], w_lo[:, 128:] = split(w_neigh[...])
 
     for k in (1, 3, 2):
         b_x(k).wait_recv()
         b_d(k).start()
     a_z(3, 0, 0).wait_recv()
-    a_d(4, 0, 0).start()
+    a_d(4, 0).start()
     a_z(3, 1, 1).wait_recv()
-    a_d(4, 1, 1).start()
-    a_d(0, 0, 0).wait_recv()
-    a_d(0, 0, 1).wait_recv()
+    a_d(4, 1).start()
+    a_d(0, 0).wait_recv()
     for step in range(1, 4):
         for way in range(2):
-            for sub in range(2):
-                a_d(step, way, sub).wait_recv()
+            a_d(step, way).wait_recv()
     loop(0, NX, lambda k: b_d(k).wait_recv())
-    a_d(4, 0, 0).wait_recv()
-    a_d(4, 1, 1).wait_recv()
+    a_d(4, 0).wait_recv()
+    a_d(4, 1).wait_recv()
     loads[0].wait()
     loads[2].wait()
     loads[6].wait()
     loads[8].wait()
+
+    loop(1, NZ, lambda k: r_z(k).wait_recv())
+    loop(1, NX, lambda k: r_x(k).start())
+    r_d(0).start()
 
     def pack(group):
         gx = group // 4
@@ -282,11 +280,11 @@
         base = pl.multiple_of(group * 144, 16)
         left = [wa[cc, gz + dz, gx].astype(F32) for dz in range(2) for cc in range(2)]
         right = [wb[cc, gx, gz + dz].astype(F32) for dz in range(2) for cc in range(2)]
-        for i in range(3):
-            rows = slice(i * WIDE, (i + 1) * WIDE)
-            for start, pieces in ((0, left), (HALF, right)):
-                column = jnp.concatenate([piece[rows] for piece in pieces], axis=0)
-                dense[pl.ds(base, 144), start + i * 128:start + (i + 1) * 128] = column.astype(BF16)
+        for i in range(6):
+            pieces = left if i < 2 else right
+            first = (i if i < 2 else i - 2) * WIDE
+            column = jnp.concatenate([piece[first:first + WIDE] for piece in pieces], axis=0)
+            dense[pl.ds(base, 144), i * 128:(i + 1) * 128] = column.astype(BF16)
 
     loop(0, 16, pack)
 
@@ -302,6 +300,9 @@
         vals[block] = dot(texts[...], dense[rows, :], NT).astype(BF16).reshape(TITLES, SEQ, 256)
 
     loop(0, 3, project)
+
+    loop(1, NX, lambda k: r_x(k).wait_recv())
+    loop(1, NX, lambda k: r_d(k).start())
 
     adder = jnp.where((iota((8, 4 * SEQ), 1) // SEQ) == (iota((8, 4 * SEQ), 0) % 4), 1.0, 0.0).astype(BF16)
     upper = iota((8, SEQ), 0) < 4
@@ -343,7 +344,13 @@
     variance = jnp.mean((means - center) ** 2, axis=1, keepdims=True)
     feats[y] = ((means - center) / jnp.sqrt(variance + 1e-05) * gain[...]).astype(BF16)
 
-    loop(1, NY, lambda k: f_y(k).start())
+    for k in (4, 3, 5, 2, 6, 1, 7):
+        f_y(k).start()
+    loads[4].wait()
+    loads[5].wait()
+    w_hi[:, :128], w_lo[:, :128] = split(w_self[...])
+    w_hi[:, 128:], w_lo[:, 128:] = split(w_neigh[...])
+    count(38, 52)
     loop(0, NX, lambda k: r_d(k).wait_recv())
     title = iota((128, 512), 1)
     named = iota((128, 512), 0)
@@ -374,13 +381,18 @@
     group_feats = jnp.concatenate([feats[g].astype(F32) for g in range(NY)], axis=0).astype(BF16)
     tg[x, c, z] = (dot(group_feats, w_hi[...]) + dot(group_feats, w_lo[...])).astype(BF16)
 
-    for k in (1, 7, 2, 6, 3, 5, 4):
+    for k in (4, 3, 5):
         t_z(k).start()
-    loop(1, NX, lambda k: t_s(k, 0).start())
+    for k in range(1, NX):
+        t_s(k, 0).start()
+    for k in (2, 6, 1, 7):
+        t_z(k).start()
+    count(52, 64)
     loop(0, 16, flip)
     for k in (1, 7, 2, 6, 3, 5, 4):
         t_z(k).wait_recv()
-        loop(1, NX, lambda n: t_s(n, NZ - k).start())
+        for n in range(1, NX):
+            t_s(n, NZ - k).start()
     t_d(0).start()
 
     def place(block):
@@ -398,19 +410,21 @@
         place((x - k + NX) % NX)
 
     def layer(step):
-        rows = pl.ds(pl.multiple_of(step * 256, 256), 256)
+        rows = pl.ds(step * 256, 256)
         total = xs[rows, :128].astype(F32) + dot(adj[rows, :], xs[:, 128:]) + bias[...]
         gate = 1.0 / (1.0 + jnp.exp(-total))
         hidden_out[rows, :] = total * gate
         ds[rows, :128] = (cot[rows, :] * gate * (1.0 + total * (1.0 - gate))).astype(BF16)
 
-    loop(0, 4, layer)
+    for step in range(4):
+        layer(step)
 
     def backward(step):
-        rows = pl.ds(pl.multiple_of(step * 256, 256), 256)
+        rows = pl.ds(step * 256, 256)
         ds[rows, 128:] = dot(adj_t[rows, :], ds[:, :128]).astype(BF16)
 
-    loop(0, 4, backward)
+    for step in range(4):
+        backward(step)
 
     def titles_of(block):
         rows = jnp.concatenate(
@@ -425,7 +439,8 @@
         to = (x + k) % NX
         u_d(k).wait_recv()
         vs[to] = (ub[to, c].astype(F32) + ur[to].astype(F32)).astype(BF16).reshape(NZ, 32, COLS)
-        loop(0, NZ, lambda dz: u_x(k, (dz + 4) % NZ).start())
+        for dz in (4, 5, 3, 6, 2, 7, 1, 0):
+            u_x(k, dz).start()
     u_d(0).wait_recv()
     vs[x] = (ub[x, c].astype(F32) + ur[x].astype(F32)).astype(BF16).reshape(NZ, 32, COLS)
 
@@ -447,7 +462,8 @@
     partial = dot(high, w_hi[...], NT) + dot(high, w_lo[...], NT) + dot(low, w_hi[...], NT)
     for g in range(NY):
         po[g] = partial[g * 4:(g + 1) * 4].astype(BF16)
-    loop(1, NY, lambda k: p_y(k).start())
+    for k in (4, 3, 5, 2, 6, 1, 7):
+        p_y(k).start()
     result = po[y].astype(F32)
     for k in range(1, NY):
         p_y(k).wait_recv()
@@ -476,13 +492,10 @@
             for sub in range(2):
                 if step < 3 or way == sub:
                     a_z(step, way, sub).wait_send()
-    a_d(0, 0, 0).wait_send()
-    a_d(0, 0, 1).wait_send()
+    a_d(0, 0).wait_send()
     for step in range(1, 5):
         for way in range(2):
-            for sub in range(2):
-                if step < 4 or way == sub:
-                    a_d(step, way, sub).wait_send()
+            a_d(step, way).wait_send()
 
 
 def shards(texts, qkv_weight, norm_gain, routes, w_self, w_neigh, gnn_bias, neighbors, cotangent):
@@ -507,8 +520,8 @@
             pltpu.VMEM((FAN, ROWS), jnp.int32),
             pltpu.VMEM((ROWS, 128), F32),
             dma((9,)),
-            pltpu.VMEM((NC, NZ, NX, PIECE, 128), BF16),
-            pltpu.VMEM((NC, NX, NZ, PIECE, 128), BF16),
+            pltpu.VMEM((NC, NZ, NX, PIECE_A, 128), BF16),
+            pltpu.VMEM((NC, NX, NZ, PIECE_B, 128), BF16),
             pltpu.VMEM((3 * D, D), BF16),
             pltpu.VMEM((3, TITLES, 256, SEQ), BF16),
             pltpu.VMEM((3, TITLES, SEQ, 256), BF16),
@@ -536,7 +549,7 @@
             pltpu.VMEM((NY, TITLES, D), BF16),
             dma((NX,)), dma((NX,)),
             dma((4, 2, 2)), dma((4, 2, 2)),
-            dma((5, 2, 2)), dma((5, 2, 2)),
+            dma((5, 2)), dma((5, 2)),
             dma((NZ,)), dma((NZ,)),
             dma((NX,)), dma((NX,)),
             dma((NX,)), dma((NX,)),

time: 89.8 us -> 88 us (0.980)
  Pallas kernels: 85 us -> 82.4 us
    pallas_call x1, Pallas kernels: 85 us -> 82.4 us  [shards(): pl.pallas_call(kernel, out_shape=(jax.ShapeDtypeStruct((ROWS, 128), F32),...]
where the time goes in v3:
time: 88 us; the launch traced here: 86.8 us
  Pallas kernels  82.4 us (94%)
  local copies, waits for them, and re-layouts  3.74 us (4%)
    pallas_call x1, Pallas kernels, shards(): pl.pallas_call(kernel, out_shape=(jax.ShapeDtypeStruct((ROWS, 128), F32),...  82.4 us
    unnamed x6, local copies, waits for them, and re-layouts  3.16 us

profile of v3, /device:TPU:1, one launch (start us, length us, event | category | flops | bytes accessed | tf_op | source)
XLA Modules:
  0.0 86.8 jit_solution(121884434285813045)
XLA Ops:
  0.6 0.0 copy-start.1
  0.6 0.7 copy-done.1
  1.3 0.6 reshape.14.gain_in
  1.9 82.4 %glem_step.1 = (f32[1024,128]{1,0:T(8,128)}, f32[4,768]{1,0:T(4,128)}) custom-call(bf16[512,768]{1,0:T(8,128)(2,1)} %bitcast.4, bf16[36,768]{1,0:T(8,128)(2,1)} %bitcast.6, f32[1,768]{1,0:T(1,128)} %reshape.14.gain_in, s32[4,8]{1,0:T(4,128)} %routes_in.1, f32[768,128]{1,0:T(8,128)} %w_self_in.1, f32[768,128]{1,0:T(8,128)} %w_neigh_in.1, f32[1,128]{1,0:T(1,128)} %bitcast.7, ...), custom_call_target="tpu_custom_call" | custom-call | tf_op jit(solution)/shard_map/glem_step/pallas_call | solution.py:504
  84.3 0.0 copy-start
  84.3 1.9 %copy.13 = f32[1024,128]{1,0:T(8,128)} copy(f32[1024,128]{1,0:T(8,128)} %get-tuple-element.4) | data formatting | bytes 1048576
  86.2 0.0 copy-done
  86.2 0.6 copy.14
Async XLA Ops:
  0.6 0.7 copy-start.1
  84.3 1.9 %copy-start = (f32[4,768]{1,0:T(4,128)S(1)}, f32[4,768]{1,0:T(4,128)}, u32[]{:S(2)}) copy-start(f32[4,768]{1,0:T(4,128)} %get-tuple-element.5) | copy-start | bytes 36868

commit v4 on v3

--- a/solution.py
+++ b/solution.py
@@ -242,10 +242,10 @@
     pass_a(0)
     pass_b(3)
     pass_b(5)
+    pass_a(1)
     pass_b(4)
     b_d(0).start()
     count(32, 38)
-    pass_a(1)
     loop(1, NY, lambda k: r_y(k).wait_recv())
     rt[x, c, z] = jnp.sum(ry[...], axis=0)
     loop(1, NZ, lambda k: r_z(k).start())
@@ -387,13 +387,13 @@
         t_s(k, 0).start()
     for k in (2, 6, 1, 7):
         t_z(k).start()
-    count(52, 64)
-    loop(0, 16, flip)
     for k in (1, 7, 2, 6, 3, 5, 4):
         t_z(k).wait_recv()
         for n in range(1, NX):
             t_s(n, NZ - k).start()
     t_d(0).start()
+    count(52, 64)
+    loop(0, 16, flip)
 
     def place(block):
         rows = dot(sel[block], tg[block].reshape(512, COLS)).astype(BF16)

time: 88 us -> 88 us (level)
  no operation moved by 1% of the time
where the time goes in v4:
time: 88 us; the launch traced here: 86.5 us
  Pallas kernels  82.1 us (93%)
  local copies, waits for them, and re-layouts  3.74 us (4%)
    pallas_call x1, Pallas kernels, shards(): pl.pallas_call(kernel, out_shape=(jax.ShapeDtypeStruct((ROWS, 128), F32),...  82.1 us
    unnamed x6, local copies, waits for them, and re-layouts  3.16 us

profile of v4, /device:TPU:1, one launch (start us, length us, event | category | flops | bytes accessed | tf_op | source)
XLA Modules:
  0.0 86.5 jit_solution(7611208820113944597)
XLA Ops:
  0.6 0.0 copy-start.1
  0.6 0.7 copy-done.1
  1.3 0.6 reshape.14.gain_in
  1.9 82.1 %glem_step.1 = (f32[1024,128]{1,0:T(8,128)}, f32[4,768]{1,0:T(4,128)}) custom-call(bf16[512,768]{1,0:T(8,128)(2,1)} %bitcast.4, bf16[36,768]{1,0:T(8,128)(2,1)} %bitcast.6, f32[1,768]{1,0:T(1,128)} %reshape.14.gain_in, s32[4,8]{1,0:T(4,128)} %routes_in.1, f32[768,128]{1,0:T(8,128)} %w_self_in.1, f32[768,128]{1,0:T(8,128)} %w_neigh_in.1, f32[1,128]{1,0:T(1,128)} %bitcast.7, ...), custom_call_target="tpu_custom_call" | custom-call | tf_op jit(solution)/shard_map/glem_step/pallas_call | solution.py:504
  84.0 0.0 copy-start
  84.0 1.9 %copy.13 = f32[1024,128]{1,0:T(8,128)} copy(f32[1024,128]{1,0:T(8,128)} %get-tuple-element.4) | data formatting | bytes 1048576
  85.9 0.0 copy-done
  85.9 0.6 copy.14
Async XLA Ops:
  0.6 0.7 copy-start.1
  84.0 1.9 %copy-start = (f32[4,768]{1,0:T(4,128)S(1)}, f32[4,768]{1,0:T(4,128)}, u32[]{:S(2)}) copy-start(f32[4,768]{1,0:T(4,128)} %get-tuple-element.5) | copy-start | bytes 36868
